TPU v7x, 32 devices: a whole 2x2x4 slice. The times are simulated.
32 devices in a mesh: dp: 4 (over y, core), expert: 8 (over z, x).
Axes of the slice: x: 2, y: 2, z: 4, core: 2. Of those that a mesh axis runs over, the one named last changes fastest.
Arguments:
- feats: bfloat16 [4, 32, 128, 512], P('dp', 'expert'), may hold values from -6 to 6
- labels: int32 [4, 32, 128, 1], P('dp', 'expert'), may hold values from 0 to 7; in each aligned block of 512 rows (0 to 511, 512 to 1023, ..., all dimensions but the last counted through in order) at most 128 rows name the same one
- w_first: bfloat16 [8, 512, 2048], P('expert'), may hold values from -0.25 to 0.25
- w_second: bfloat16 [8, 2048, 256], P('expert'), may hold values from -0.125 to 0.125
- kernel: bfloat16 [27, 256, 256], replicated, may hold values from -0.078125 to 0.078125
- cotangent: bfloat16 [4, 32, 128, 256], P('dp', 'expert'), may hold values from -6 to 6
Outputs:
- imitated: bfloat16 [4, 32, 128, 256], P('dp', 'expert')
- feat_grad: bfloat16 [4, 32, 128, 512], P('dp', 'expert')
- grad_first: float32 [8, 512, 2048], P('expert', None, 'dp')
- grad_second: float32 [8, 2048, 256], P('expert', 'dp')
Inputs may be any that keep to these rules, and one draw needn't show every extreme that they name: `labels`: within the 512 patches of one device (aligned blocks of 512 patches in grid order), no label occurs more than 128 times, and some label occurs exactly 128 times.
All inputs are finite; a program needn't handle non-finite values.
Results may differ from a plain program's by a relative error of at most 0.023.
Values may be sent and summed in bfloat16 or wider, within the bound.
A program may use at most 128 MiB of HBM per device.

v0:
```python
import functools

import jax
import jax.numpy as jnp
from jax import lax
from jax.experimental import pallas as pl
from jax.experimental.pallas import tpu as pltpu
from jax.sharding import PartitionSpec as P

BF16 = jnp.bfloat16
F32 = jnp.float32
ROOT = 0.7978845608028654
CUBIC = 0.044715


def dot(a, b):
    return jnp.dot(a, b, preferred_element_type=F32)


def dot_t(a, b):
    return lax.dot_general(a, b, (((1,), (1,)), ((), ())), preferred_element_type=F32)


def remote(src, dst, send, recv, **device):
    return pltpu.make_async_remote_copy(
        src_ref=src,
        dst_ref=dst,
        send_sem=send,
        recv_sem=recv,
        device_id=device,
        device_id_type=pl.DeviceIdType.MESH,
    )


def shifted(value, step, depth):
    rows = value.shape[0]
    place = lax.broadcasted_iota(jnp.int32, value.shape, 0) % depth
    if step > 0:
        return jnp.where(place == 0, 0.0, pltpu.roll(value, 1, 0))
    return jnp.where(place == depth - 1, 0.0, pltpu.roll(value, rows - 1, 0))


def convolved(grid, taps, rows, depth, flipped):
    channels = taps.shape[1]
    tokens = rows * depth
    pieces, sums = [], []
    for a in range(3):
        for b in range(3):
            at, bt = (2 - a, 2 - b) if flipped else (a, b)
            pieces.append(grid[bt : bt + rows, at].reshape(tokens, channels))
    columns = jnp.concatenate(pieces, axis=1)
    for c in range(3):
        if flipped:
            weights = jnp.concatenate([taps[3 * k + c] for k in range(9)], axis=1)
            sums.append(dot_t(columns, weights))
        else:
            weights = jnp.concatenate([taps[3 * k + c] for k in range(9)], axis=0)
            sums.append(dot(columns, weights))
    first, last = (sums[2], sums[0]) if flipped else (sums[0], sums[2])
    return sums[1] + shifted(first, 1, depth) + shifted(last, -1, depth)


def kernel(
    n_dp, n_ex,
    labels, feats, cot, w1_hbm, w2_hbm, taps_hbm,
    imitated, feat_grad, grad_one, grad_two,
    w1, w2, taps, spread,
    out_f, in_f, out_g, in_g, out_o, in_o, out_b, in_b,
    act, slope, gate, grid_g, grid_o,
    part1, part2, pair1, pair2, sum1, sum2, far1, far2,
    load_sem, halo_send, halo_recv,
    f_send, f_recv, g_send, g_recv, o_send, o_recv, b_send, b_recv,
    pair_send, pair_recv, far_send, far_recv,
):
    tokens, width = feats.shape
    rows, depth, channels = cot.shape
    hidden = w1.shape[1]
    cap = in_f.shape[1]
    slots = n_ex * cap
    block = hidden // n_dp
    half = n_dp // 2
    dp = lax.axis_index("dp")
    me = lax.axis_index("expert")
    side = dp % 2
    level = dp // 2
    mate = dp + 1 - 2 * side

    loads = [
        pltpu.make_async_copy(w1_hbm, w1, load_sem.at[0]),
        pltpu.make_async_copy(w2_hbm, w2, load_sem.at[1]),
        pltpu.make_async_copy(taps_hbm, taps, load_sem.at[2]),
    ]
    loads[2].start()
    loads[0].start()
    loads[1].start()

    barrier = pltpu.get_barrier_semaphore()

    def greet_expert(d, carry):
        pl.semaphore_signal(
            barrier, inc=1, device_id={"expert": (me + d) % n_ex},
            device_id_type=pl.DeviceIdType.MESH,
        )
        return carry

    def greet_dp(d, carry):
        pl.semaphore_signal(
            barrier, inc=1, device_id={"dp": (dp + d) % n_dp},
            device_id_type=pl.DeviceIdType.MESH,
        )
        return carry

    lax.fori_loop(1, n_ex, greet_expert, 0)
    lax.fori_loop(1, n_dp, greet_dp, 0)
    grid_g[1 : rows + 1, 1] = cot[...]

    relative = labels[...] - me
    relative = jnp.where(relative < 0, relative + n_ex, relative)
    relative = jnp.where(
        relative >= n_ex // 2, 2 * relative - n_ex, n_ex - 1 - 2 * relative)
    named = lax.broadcasted_iota(jnp.int32, (n_ex, tokens), 0)
    hot = relative == named
    before = (
        lax.broadcasted_iota(jnp.int32, (tokens, tokens), 0)
        < lax.broadcasted_iota(jnp.int32, (tokens, tokens), 1)
    )
    rank = dot(jnp.where(hot, 1.0, 0.0).astype(BF16), jnp.where(before, 1.0, 0.0).astype(BF16))
    place = rank + (named * cap).astype(F32)
    target = jnp.sum(jnp.where(hot, place, 0.0), axis=0, keepdims=True)
    which = lax.broadcasted_iota(jnp.int32, (cap, tokens), 0)

    def halo(grid, at):
        return (
            (me < n_ex - 1, me > 0, remote(
                grid.at[rows, 1], grid.at[0, 1],
                halo_send.at[at], halo_recv.at[at], expert=(me + 1) % n_ex)),
            (me > 0, me < n_ex - 1, remote(
                grid.at[1, 1], grid.at[rows + 1, 1],
                halo_send.at[at + 1], halo_recv.at[at + 1], expert=(me + n_ex - 1) % n_ex)),
            (dp < n_dp - 1, dp > 0, remote(
                grid.at[:, 1], grid.at[:, 0],
                halo_send.at[at + 2], halo_recv.at[at + 2], dp=(dp + 1) % n_dp)),
            (dp > 0, dp < n_dp - 1, remote(
                grid.at[:, 1], grid.at[:, 2],
                halo_send.at[at + 3], halo_recv.at[at + 3], dp=(dp + n_dp - 1) % n_dp)),
        )

    def begin(steps):
        for sends, _, copy in steps:
            pl.when(sends)(copy.start)

    def landed(steps):
        for _, gets, copy in steps:
            pl.when(gets)(copy.wait_recv)

    def finish(steps):
        for sends, _, copy in steps:
            pl.when(sends)(copy.wait_send)

    def edges(grid):
        slab = jnp.zeros((rows + 2, depth, channels), BF16)
        strip = jnp.zeros((depth, channels), BF16)

        @pl.when(dp == 0)
        def _():
            grid[:, 0] = slab

        @pl.when(dp == n_dp - 1)
        def _():
            grid[:, 2] = slab

        @pl.when(me == 0)
        def _():
            grid[0, 1] = strip

        @pl.when(me == n_ex - 1)
        def _():
            grid[rows + 1, 1] = strip

    halo_g, halo_o = halo(grid_g, 0), halo(grid_o, 4)
    pl.semaphore_wait(barrier, n_ex + n_dp - 2)
    begin(halo_g[:2])

    def turn(i):
        return n_ex // 2 + (1 - 2 * (i % 2)) * ((i + 1) // 2)

    def outward(src, dst, send, recv, i):
        return remote(
            src.at[i], dst.at[i], send.at[i], recv.at[i], expert=(me + turn(i)) % n_ex
        )

    def homeward(src, dst, send, recv, i):
        return remote(
            src.at[i], dst.at[i], send.at[i], recv.at[i], expert=(me + n_ex - turn(i)) % n_ex
        )

    def chosen(i):
        hit = (which + i * cap).astype(F32) == target
        return jnp.where(hit, 1.0, 0.0).astype(BF16)

    def send_feats(i, carry):
        spread[i] = chosen(i)
        out_f[i] = dot(spread[i], feats[...]).astype(BF16)
        outward(out_f, in_f, f_send, f_recv, i).start()
        return carry

    own = n_ex - 1
    lax.fori_loop(0, 2, send_feats, 0)
    edges(grid_g)
    landed(halo_g[:2])
    begin(halo_g[2:])
    lax.fori_loop(2, own, send_feats, 0)
    spread[own] = chosen(own)
    in_f[own] = dot(spread[own], feats[...]).astype(BF16)

    tile = min(hidden, 512)
    loads[2].wait()
    landed(halo_g[2:])
    field_grad = convolved(grid_g, taps, rows, depth, True).astype(BF16)
    grid_o[1 : rows + 1, 1] = field_grad.reshape(rows, depth, channels)

    def send_grads(i, carry):
        out_g[i] = dot(spread[i], grid_o[1 : rows + 1, 1].reshape(tokens, channels)).astype(BF16)
        outward(out_g, in_g, g_send, g_recv, i).start()
        return carry

    lax.fori_loop(0, own, send_grads, 0)
    in_g[own] = dot(spread[own], grid_o[1 : rows + 1, 1].reshape(tokens, channels)).astype(BF16)
    finish(halo_g)
    loads[0].wait()
    loads[1].wait()

    def forward(k):
        both = pl.ds(2 * k, 2)
        row_block = in_f[both].reshape(2 * cap, width)
        for at in range(0, hidden, tile):
            v = dot(row_block, w1[:, at : at + tile])
            square = v * v
            t = jnp.tanh(v * (ROOT + (ROOT * CUBIC) * square))
            half_up = 0.5 + 0.5 * t
            act[both, :, at : at + tile] = (v * half_up).astype(BF16).reshape(2, cap, tile)
            inner = ROOT + (3.0 * ROOT * CUBIC) * square
            grown = half_up + (0.5 * v) * (1.0 - t * t) * inner
            slope[both, :, at : at + tile] = grown.reshape(2, cap, tile)
        result = dot(act[both].reshape(2 * cap, hidden), w2[...])
        out_o[both] = result.astype(BF16).reshape(2, cap, channels)

    def go_forward(k, carry):
        for i in (2 * k, 2 * k + 1):
            outward(out_f, in_f, f_send, f_recv, i).wait_recv()
        forward(k)
        for i in (2 * k, 2 * k + 1):
            homeward(out_o, in_o, o_send, o_recv, i).start()
        return carry

    pairs = n_ex // 2
    lax.fori_loop(0, pairs - 1, go_forward, 0)
    outward(out_f, in_f, f_send, f_recv, own - 1).wait_recv()
    forward(pairs - 1)
    homeward(out_o, in_o, o_send, o_recv, own - 1).start()
    in_o[own] = out_o[own]

    def backward(k):
        both = pl.ds(2 * k, 2)
        grads = in_g[both].reshape(2 * cap, channels)
        for at in range(0, hidden, tile):
            up = dot_t(grads, w2[at : at + tile, :])
            scale = slope[both, :, at : at + tile].reshape(2 * cap, tile)
            gate[both, :, at : at + tile] = (up * scale).astype(BF16).reshape(2, cap, tile)
        result = dot_t(gate[both].reshape(2 * cap, hidden), w1[...])
        out_b[both] = result.astype(BF16).reshape(2, cap, width)

    def go_backward(k, carry):
        for i in (2 * k, 2 * k + 1):
            outward(out_g, in_g, g_send, g_recv, i).wait_recv()
        backward(k)
        for i in (2 * k, 2 * k + 1):
            homeward(out_b, in_b, b_send, b_recv, i).start()
        return carry

    lax.fori_loop(0, pairs // 2, go_backward, 0)

    def got_outs(i, carry):
        homeward(out_o, in_o, o_send, o_recv, i).wait_recv()
        return carry

    lax.fori_loop(0, own, got_outs, 0)
    back = spread[...].reshape(slots, tokens).T
    mixed = dot(back, in_o[...].reshape(slots, channels)).astype(BF16)
    grid_o[1 : rows + 1, 1] = mixed.reshape(rows, depth, channels)
    begin(halo_o[:2])
    edges(grid_o)
    lax.fori_loop(pairs // 2, pairs - 1, go_backward, 0)
    outward(out_g, in_g, g_send, g_recv, own - 1).wait_recv()
    backward(pairs - 1)
    homeward(out_b, in_b, b_send, b_recv, own - 1).start()
    in_b[own] = out_b[own]
    landed(halo_o[:2])
    begin(halo_o[2:])

    feats_t = in_f[...].reshape(slots, width).T
    grads_t = in_g[...].reshape(slots, channels).T
    pair = {}
    for o in list(range(1, half)) + [0]:
        other = (level + o) % half
        for parity in range(2):
            start = pl.multiple_of((2 * other + parity) * block, block)
            part1[parity, other] = dot(
                feats_t, gate[:, :, pl.ds(start, block)].reshape(slots, block)).astype(BF16)
            part2[parity, other] = dot(
                grads_t, act[:, :, pl.ds(start, block)].reshape(slots, block)).astype(BF16)
        pair[o] = (
            remote(part1.at[1 - side, other], pair1.at[o],
                   pair_send.at[0, o], pair_recv.at[0, o], dp=mate),
            remote(part2.at[1 - side, other], pair2.at[o],
                   pair_send.at[1, o], pair_recv.at[1, o], dp=mate),
        )
        for copy in pair[o]:
            copy.start()
    far = []
    for o in range(1, half):
        other = (level + o) % half
        for copy in pair[o]:
            copy.wait()
        sum1[o] = (part1[side, other].astype(F32) + pair1[o].astype(F32)).astype(BF16)
        sum2[o] = (part2[side, other].astype(F32) + pair2[o].astype(F32)).astype(BF16)
        to = 2 * other + side
        far.append(remote(
            sum1.at[o], far1.at[o], far_send.at[0, o], far_recv.at[0, o], dp=to))
        far.append(remote(
            sum2.at[o], far2.at[o], far_send.at[1, o], far_recv.at[1, o], dp=to))
        far[-2].start()
        far[-1].start()
    landed(halo_o[2:])
    imitated[...] = convolved(grid_o, taps, rows, depth, False).astype(BF16)
    finish(halo_o)
    for copy in pair[0]:
        copy.wait()
    for copy in far:
        copy.wait()
    total1 = part1[side, level].astype(F32) + pair1[0].astype(F32)
    total2 = part2[side, level].astype(F32) + pair2[0].astype(F32)
    for o in range(1, half):
        total1 = total1 + far1[o].astype(F32)
        total2 = total2 + far2[o].astype(F32)
    grad_one[...] = total1
    grad_two[...] = total2.T

    def got_back(i, carry):
        homeward(out_b, in_b, b_send, b_recv, i).wait_recv()
        return carry

    lax.fori_loop(0, own, got_back, 0)
    feat_grad[...] = dot(back, in_b[...].reshape(slots, width)).astype(BF16)

    def drained(i, carry):
        outward(out_f, in_f, f_send, f_recv, i).wait_send()
        outward(out_g, in_g, g_send, g_recv, i).wait_send()
        homeward(out_o, in_o, o_send, o_recv, i).wait_send()
        homeward(out_b, in_b, b_send, b_recv, i).wait_send()
        return carry

    lax.fori_loop(0, own, drained, 0)


def handed_on(*refs):
    count = len(refs) // 2
    sems = refs[-1]
    copies = [
        pltpu.make_async_copy(refs[i], refs[count + i], sems.at[i]) for i in range(count)
    ]
    for copy in copies:
        copy.start()
    for copy in copies:
        copy.wait()


def per_device(feats, labels, w_first, w_second, taps, cotangent):
    n_dp = lax.axis_size("dp")
    n_ex = lax.axis_size("expert")
    rows, depth, width = feats.shape[1:]
    channels = taps.shape[2]
    hidden = w_first.shape[2]
    tokens = rows * depth
    cap = 2 * tokens // n_ex
    block = hidden // n_dp
    half = n_dp // 2
    vmem = pl.BlockSpec(memory_space=pltpu.VMEM)
    hbm = pl.BlockSpec(memory_space=pl.ANY)
    wide = pltpu.VMEM((n_ex, cap, width), BF16)
    thin = pltpu.VMEM((n_ex, cap, channels), BF16)
    grid = pltpu.VMEM((rows + 2, 3, depth, channels), BF16)
    dma = pltpu.SemaphoreType.DMA
    outs = pl.pallas_call(
        functools.partial(kernel, n_dp, n_ex),
        out_shape=(
            jax.ShapeDtypeStruct((tokens, channels), BF16),
            jax.ShapeDtypeStruct((tokens, width), BF16),
            jax.ShapeDtypeStruct((width, block), F32),
            jax.ShapeDtypeStruct((block, channels), F32),
        ),
        in_specs=[vmem, vmem, vmem, hbm, hbm, hbm],
        out_specs=(vmem,) * 4,
        scratch_shapes=[
            pltpu.VMEM((width, hidden), BF16),
            pltpu.VMEM((hidden, channels), BF16),
            pltpu.VMEM(taps.shape, BF16),
            pltpu.VMEM((n_ex, cap, tokens), BF16),
            wide, wide, thin, thin, thin, thin, wide, wide,
            pltpu.VMEM((n_ex, cap, hidden), BF16),
            pltpu.VMEM((n_ex, cap, hidden), F32),
            pltpu.VMEM((n_ex, cap, hidden), BF16),
            grid, grid,
            pltpu.VMEM((2, half, width, block), BF16),
            pltpu.VMEM((2, half, channels, block), BF16),
            pltpu.VMEM((half, width, block), BF16),
            pltpu.VMEM((half, channels, block), BF16),
            pltpu.VMEM((half, width, block), BF16),
            pltpu.VMEM((half, channels, block), BF16),
            pltpu.VMEM((half, width, block), BF16),
            pltpu.VMEM((half, channels, block), BF16),
            dma((3,)), dma((8,)), dma((8,)),
            dma((n_ex,)), dma((n_ex,)), dma((n_ex,)), dma((n_ex,)),
            dma((n_ex,)), dma((n_ex,)), dma((n_ex,)), dma((n_ex,)),
            dma((2, half)), dma((2, half)), dma((2, half)), dma((2, half)),
        ],
        compiler_params=pltpu.CompilerParams(
            collective_id=0, has_side_effects=True, vmem_limit_bytes=60 * 2**20
        ),
        name="routed_experts",
    )(
        labels.reshape(1, tokens),
        feats.reshape(tokens, width),
        cotangent.reshape(rows, depth, channels),
        w_first[0],
        w_second[0],
        taps,
    )
    imitated, feat_grad, grad_one, grad_two = pl.pallas_call(
        handed_on,
        out_shape=tuple(jax.ShapeDtypeStruct(x.shape, x.dtype) for x in outs),
        in_specs=[hbm] * 4,
        out_specs=(hbm,) * 4,
        scratch_shapes=[dma((4,))],
        compiler_params=pltpu.CompilerParams(vmem_limit_bytes=60 * 2**20),
        name="handed_on",
    )(*outs)
    return (
        imitated.reshape(1, rows, depth, channels),
        feat_grad.reshape(1, rows, depth, width),
        grad_one[None],
        grad_two[None],
    )


def solution(mesh):
    in_specs = (
        P("dp", "expert", None, None),
        P("dp", "expert", None, None),
        P("expert", None, None),
        P("expert", None, None),
        P(),
        P("dp", "expert", None, None),
    )
    out_specs = (
        P("dp", "expert", None, None),
        P("dp", "expert", None, None),
        P("expert", None, "dp"),
        P("expert", "dp", None),
    )
    return jax.shard_map(
        per_device, mesh=mesh, in_specs=in_specs, out_specs=out_specs, check_vma=False
    )
```

profile of v0, /device:TPU:10, one launch (start us, length us, event | category | flops | bytes accessed | tf_op | source)
XLA Modules:
  0.0 177.8 jit_solution(6004468739132409611)
XLA Ops:
  0.6 104.4 %routed_experts.1 = (bf16[512,256]{1,0:T(8,128)(2,1)}, bf16[512,512]{1,0:T(8,128)(2,1)}, f32[512,512]{1,0:T(8,128)}, f32[512,256]{1,0:T(8,128)}) custom-call(s32[1,512]{1,0:T(1,128)} %bitcast.13, bf16[512,512]{1,0:T(8,128)(2,1)} %bitcast.11, bf16[4,128,256]{2,1,0:T(8,128)(2,1)} %bitcast.12, bf16[512,2048]{1,0:T(8,128)(2,1)} %bitcast.9, ...), custom_call_target="tpu_custom_call" | custom-call | tf_op jit(solution)/shard_map/routed_experts/pallas_call | solution.py:394
  105.0 72.6 %handed_on.1 = (bf16[512,256]{1,0:T(8,128)(2,1)}, bf16[512,512]{1,0:T(8,128)(2,1)}, f32[512,512]{1,0:T(8,128)}, f32[512,256]{1,0:T(8,128)}) custom-call(bf16[512,256]{1,0:T(8,128)(2,1)} %get-tuple-element.12.refs_0_, bf16[512,512]{1,0:T(8,128)(2,1)} %get-tuple-element.13.refs_1_, f32[512,512]{1,0:T(8,128)} %get-tuple-element.14.refs_2_, ...), custom_call_target="tpu_custom_call" | custom-call | tf_op jit(solution)/shard_map/handed_on/pallas_call | solution.py:439
where the time goes:
time: 178 us
  Pallas kernels  177 us (99%)
    pallas_call x1, Pallas kernels, per_device(): pl.pallas_call(functools.partial(kernel, n_dp, n_ex), out_shape=(jax.Shap...  104 us
    pallas_call x1, Pallas kernels, per_device(): pl.pallas_call(handed_on, out_shape=tuple((jax.ShapeDtypeStruct(x.shape,...  72.6 us

commit v1 on v0

--- a/solution.py
+++ b/solution.py
@@ -270,33 +270,25 @@
         result = dot_t(gate[both].reshape(2 * cap, hidden), w1[...])
         out_b[both] = result.astype(BF16).reshape(2, cap, width)
 
+    def got_grads(i):
+        outward(out_g, in_g, g_send, g_recv, i).wait_recv()
+
+    def send_back(i, carry):
+        homeward(out_b, in_b, b_send, b_recv, i).start()
+        return carry
+
     def go_backward(k, carry):
-        for i in (2 * k, 2 * k + 1):
-            outward(out_g, in_g, g_send, g_recv, i).wait_recv()
+        got_grads(2 * k)
+        got_grads(2 * k + 1)
         backward(k)
-        for i in (2 * k, 2 * k + 1):
-            homeward(out_b, in_b, b_send, b_recv, i).start()
-        return carry
-
-    lax.fori_loop(0, pairs // 2, go_backward, 0)
-
-    def got_outs(i, carry):
-        homeward(out_o, in_o, o_send, o_recv, i).wait_recv()
-        return carry
-
-    lax.fori_loop(0, own, got_outs, 0)
-    back = spread[...].reshape(slots, tokens).T
-    mixed = dot(back, in_o[...].reshape(slots, channels)).astype(BF16)
-    grid_o[1 : rows + 1, 1] = mixed.reshape(rows, depth, channels)
-    begin(halo_o[:2])
-    edges(grid_o)
-    lax.fori_loop(pairs // 2, pairs - 1, go_backward, 0)
-    outward(out_g, in_g, g_send, g_recv, own - 1).wait_recv()
+        return carry
+
+    go_backward(0, 0)
+    lax.fori_loop(0, 2, send_back, 0)
+    lax.fori_loop(1, pairs - 1, go_backward, 0)
+    got_grads(own - 1)
     backward(pairs - 1)
-    homeward(out_b, in_b, b_send, b_recv, own - 1).start()
     in_b[own] = out_b[own]
-    landed(halo_o[:2])
-    begin(halo_o[2:])
 
     feats_t = in_f[...].reshape(slots, width).T
     grads_t = in_g[...].reshape(slots, channels).T
@@ -331,6 +323,20 @@
             sum2.at[o], far2.at[o], far_send.at[1, o], far_recv.at[1, o], dp=to))
         far[-2].start()
         far[-1].start()
+
+    def got_outs(i, carry):
+        homeward(out_o, in_o, o_send, o_recv, i).wait_recv()
+        return carry
+
+    lax.fori_loop(0, own, got_outs, 0)
+    back = spread[...].reshape(slots, tokens).T
+    mixed = dot(back, in_o[...].reshape(slots, channels)).astype(BF16)
+    grid_o[1 : rows + 1, 1] = mixed.reshape(rows, depth, channels)
+    begin(halo_o[:2])
+    lax.fori_loop(2, own, send_back, 0)
+    edges(grid_o)
+    landed(halo_o[:2])
+    begin(halo_o[2:])
     landed(halo_o[2:])
     imitated[...] = convolved(grid_o, taps, rows, depth, False).astype(BF16)
     finish(halo_o)
@@ -386,7 +392,7 @@
     block = hidden // n_dp
     half = n_dp // 2
     vmem = pl.BlockSpec(memory_space=pltpu.VMEM)
-    hbm = pl.BlockSpec(memory_space=pl.ANY)
+    hbm = pl.BlockSpec(memory_space=pltpu.HBM)
     wide = pltpu.VMEM((n_ex, cap, width), BF16)
     thin = pltpu.VMEM((n_ex, cap, channels), BF16)
     grid = pltpu.VMEM((rows + 2, 3, depth, channels), BF16)
@@ -425,7 +431,7 @@
             dma((2, half)), dma((2, half)), dma((2, half)), dma((2, half)),
         ],
         compiler_params=pltpu.CompilerParams(
-            collective_id=0, has_side_effects=True, vmem_limit_bytes=60 * 2**20
+            collective_id=0, has_side_effects=True, vmem_limit_bytes=50 * 2**20
         ),
         name="routed_experts",
     )(
@@ -439,10 +445,10 @@
     imitated, feat_grad, grad_one, grad_two = pl.pallas_call(
         handed_on,
         out_shape=tuple(jax.ShapeDtypeStruct(x.shape, x.dtype) for x in outs),
-        in_specs=[hbm] * 4,
+        in_specs=[vmem] * 4,
         out_specs=(hbm,) * 4,
         scratch_shapes=[dma((4,))],
-        compiler_params=pltpu.CompilerParams(vmem_limit_bytes=60 * 2**20),
+        compiler_params=pltpu.CompilerParams(vmem_limit_bytes=8 * 2**20),
         name="handed_on",
     )(*outs)
     return (

time: 178 us -> 92.3 us (0.52)
  the two profiles are of different devices: /device:TPU:10 before, /device:TPU:17 now
where the time goes in v1:
time: 92.3 us; the launch traced here: 92.1 us
  Pallas kernels  88.7 us (96%)
  local copies, waits for them, and re-layouts  2.67 us (3%)
    pallas_call x1, Pallas kernels, per_device(): pl.pallas_call(functools.partial(kernel, n_dp, n_ex), out_shape=(jax.Shap...  87.2 us
    unnamed x6, local copies, waits for them, and re-layouts  2.67 us

profile of v1, /device:TPU:17, one launch (start us, length us, event | category | flops | bytes accessed | tf_op | source)
XLA Modules:
  0.0 92.1 jit_solution(12154206785539938854)
XLA Ops:
  0.6 0.0 copy-start
  0.6 1.0 %copy-done = bf16[1,4,128,512]{3,2,1,0:T(8,128)(2,1)S(1)} copy-done((bf16[1,4,128,512]{3,2,1,0:T(8,128)(2,1)S(1)}, bf16[1,4,128,512]{3,2,1,0:T(8,128)(2,1)}, u32[]{:S(2)}) %copy-start) | copy-done | bytes 524312
  1.7 0.0 copy-start.1
  1.7 0.9 %copy-done.1 = bf16[1,4,128,256]{3,2,1,0:T(8,128)(2,1)S(1)} copy-done((bf16[1,4,128,256]{3,2,1,0:T(8,128)(2,1)S(1)}, bf16[1,4,128,256]{3,2,1,0:T(8,128)(2,1)}, u32[]{:S(2)}) %copy-start.1) | copy-done | bytes 262168
  2.6 0.0 copy-start.2
  2.6 0.7 copy-done.2
  3.3 87.2 %routed_experts.1 = (bf16[512,256]{1,0:T(8,128)(2,1)S(1)}, bf16[512,512]{1,0:T(8,128)(2,1)S(1)}, f32[512,512]{1,0:T(8,128)S(1)}, f32[512,256]{1,0:T(8,128)S(1)}) custom-call(s32[1,512]{1,0:T(1,128)S(1)} %bitcast.11, bf16[512,512]{1,0:T(8,128)(2,1)S(1)} %bitcast.9, bf16[4,128,256]{2,1,0:T(8,128)(2,1)S(1)} %bitcast.10, bf16[512,2048]{1,0:T(8,128)(2,1)} %bitcast.12, ...), custom_call_target="tpu_custom_call" | custom-call | tf_op jit(solution)/shard_map/routed_experts/pallas_call | solution.py:400
  90.5 1.4 %handed_on.1 = (bf16[512,256]{1,0:T(8,128)(2,1)}, bf16[512,512]{1,0:T(8,128)(2,1)}, f32[512,512]{1,0:T(8,128)}, f32[512,256]{1,0:T(8,128)}) custom-call(bf16[512,256]{1,0:T(8,128)(2,1)S(1)} %get-tuple-element.12.refs_0_, bf16[512,512]{1,0:T(8,128)(2,1)S(1)} %get-tuple-element.13.refs_1_, f32[512,512]{1,0:T(8,128)S(1)} %get-tuple-element.14.refs_2_, ...), custom_call_target="tpu_custom_call" | custom-call | tf_op jit(solution)/shard_map/handed_on/pallas_call | solution.py:445
Async XLA Ops:
  0.6 1.0 %copy-start = (bf16[1,4,128,512]{3,2,1,0:T(8,128)(2,1)S(1)}, bf16[1,4,128,512]{3,2,1,0:T(8,128)(2,1)}, u32[]{:S(2)}) copy-start(bf16[1,4,128,512]{3,2,1,0:T(8,128)(2,1)} %param.6) | copy-start | bytes 1572868
  1.7 0.9 %copy-start.1 = (bf16[1,4,128,256]{3,2,1,0:T(8,128)(2,1)S(1)}, bf16[1,4,128,256]{3,2,1,0:T(8,128)(2,1)}, u32[]{:S(2)}) copy-start(bf16[1,4,128,256]{3,2,1,0:T(8,128)(2,1)} %param.11) | copy-start | bytes 786436
  2.6 0.7 copy-start.2

commit v2 on v1

--- a/solution.py
+++ b/solution.py
@@ -62,18 +62,19 @@
 
 def kernel(
     n_dp, n_ex,
-    labels, feats, cot, w1_hbm, w2_hbm, taps_hbm,
+    labels_hbm, feats_hbm, cot_hbm, w1_hbm, w2_hbm, taps_hbm,
+    imitated_hbm, feat_grad_hbm, grad_one_hbm, grad_two_hbm,
     imitated, feat_grad, grad_one, grad_two,
-    w1, w2, taps, spread,
+    labels, feats, w1, w2, taps, spread,
     out_f, in_f, out_g, in_g, out_o, in_o, out_b, in_b,
     act, slope, gate, grid_g, grid_o,
     part1, part2, pair1, pair2, sum1, sum2, far1, far2,
-    load_sem, halo_send, halo_recv,
+    load_sem, store_sem, halo_send, halo_recv,
     f_send, f_recv, g_send, g_recv, o_send, o_recv, b_send, b_recv,
     pair_send, pair_recv, far_send, far_recv,
 ):
     tokens, width = feats.shape
-    rows, depth, channels = cot.shape
+    rows, depth, channels = cot_hbm.shape
     hidden = w1.shape[1]
     cap = in_f.shape[1]
     slots = n_ex * cap
@@ -89,10 +90,19 @@
         pltpu.make_async_copy(w1_hbm, w1, load_sem.at[0]),
         pltpu.make_async_copy(w2_hbm, w2, load_sem.at[1]),
         pltpu.make_async_copy(taps_hbm, taps, load_sem.at[2]),
+        pltpu.make_async_copy(labels_hbm, labels, load_sem.at[3]),
+        pltpu.make_async_copy(cot_hbm, grid_g.at[pl.ds(1, rows), 1], load_sem.at[4]),
+        pltpu.make_async_copy(feats_hbm, feats, load_sem.at[5]),
     ]
-    loads[2].start()
-    loads[0].start()
-    loads[1].start()
+    for at in (3, 4, 5, 2, 0, 1):
+        loads[at].start()
+
+    stores = [
+        pltpu.make_async_copy(imitated, imitated_hbm, store_sem.at[0]),
+        pltpu.make_async_copy(grad_one, grad_one_hbm, store_sem.at[1]),
+        pltpu.make_async_copy(grad_two, grad_two_hbm, store_sem.at[2]),
+        pltpu.make_async_copy(feat_grad, feat_grad_hbm, store_sem.at[3]),
+    ]
 
     barrier = pltpu.get_barrier_semaphore()
 
@@ -112,7 +122,7 @@
 
     lax.fori_loop(1, n_ex, greet_expert, 0)
     lax.fori_loop(1, n_dp, greet_dp, 0)
-    grid_g[1 : rows + 1, 1] = cot[...]
+    loads[3].wait()
 
     relative = labels[...] - me
     relative = jnp.where(relative < 0, relative + n_ex, relative)
@@ -178,8 +188,10 @@
             grid[rows + 1, 1] = strip
 
     halo_g, halo_o = halo(grid_g, 0), halo(grid_o, 4)
+    loads[4].wait()
     pl.semaphore_wait(barrier, n_ex + n_dp - 2)
     begin(halo_g[:2])
+    loads[5].wait()
 
     def turn(i):
         return n_ex // 2 + (1 - 2 * (i % 2)) * ((i + 1) // 2)
@@ -249,15 +261,12 @@
         for i in (2 * k, 2 * k + 1):
             outward(out_f, in_f, f_send, f_recv, i).wait_recv()
         forward(k)
-        for i in (2 * k, 2 * k + 1):
-            homeward(out_o, in_o, o_send, o_recv, i).start()
         return carry
 
     pairs = n_ex // 2
     lax.fori_loop(0, pairs - 1, go_forward, 0)
     outward(out_f, in_f, f_send, f_recv, own - 1).wait_recv()
     forward(pairs - 1)
-    homeward(out_o, in_o, o_send, o_recv, own - 1).start()
     in_o[own] = out_o[own]
 
     def backward(k):
@@ -283,9 +292,18 @@
         backward(k)
         return carry
 
-    go_backward(0, 0)
+    def send_outs(i, carry):
+        homeward(out_o, in_o, o_send, o_recv, i).start()
+        return carry
+
+    got_grads(0)
+    got_grads(1)
+    lax.fori_loop(0, own, send_outs, 0)
+    backward(0)
     lax.fori_loop(0, 2, send_back, 0)
-    lax.fori_loop(1, pairs - 1, go_backward, 0)
+    lax.fori_loop(1, pairs // 2, go_backward, 0)
+    lax.fori_loop(2, pairs, send_back, 0)
+    lax.fori_loop(pairs // 2, pairs - 1, go_backward, 0)
     got_grads(own - 1)
     backward(pairs - 1)
     in_b[own] = out_b[own]
@@ -293,7 +311,8 @@
     feats_t = in_f[...].reshape(slots, width).T
     grads_t = in_g[...].reshape(slots, channels).T
     pair = {}
-    for o in list(range(1, half)) + [0]:
+
+    def weight_blocks(o):
         other = (level + o) % half
         for parity in range(2):
             start = pl.multiple_of((2 * other + parity) * block, block)
@@ -309,6 +328,23 @@
         )
         for copy in pair[o]:
             copy.start()
+
+    def got_outs(i, carry):
+        homeward(out_o, in_o, o_send, o_recv, i).wait_recv()
+        return carry
+
+    for o in range(1, half):
+        weight_blocks(o)
+    lax.fori_loop(0, own, got_outs, 0)
+    back = spread[...].reshape(slots, tokens).T
+    mixed = dot(back, in_o[...].reshape(slots, channels)).astype(BF16)
+    grid_o[1 : rows + 1, 1] = mixed.reshape(rows, depth, channels)
+    begin(halo_o[:2])
+    lax.fori_loop(pairs, own, send_back, 0)
+    edges(grid_o)
+    weight_blocks(0)
+    landed(halo_o[:2])
+    begin(halo_o[2:])
     far = []
     for o in range(1, half):
         other = (level + o) % half
@@ -323,22 +359,9 @@
             sum2.at[o], far2.at[o], far_send.at[1, o], far_recv.at[1, o], dp=to))
         far[-2].start()
         far[-1].start()
-
-    def got_outs(i, carry):
-        homeward(out_o, in_o, o_send, o_recv, i).wait_recv()
-        return carry
-
-    lax.fori_loop(0, own, got_outs, 0)
-    back = spread[...].reshape(slots, tokens).T
-    mixed = dot(back, in_o[...].reshape(slots, channels)).astype(BF16)
-    grid_o[1 : rows + 1, 1] = mixed.reshape(rows, depth, channels)
-    begin(halo_o[:2])
-    lax.fori_loop(2, own, send_back, 0)
-    edges(grid_o)
-    landed(halo_o[:2])
-    begin(halo_o[2:])
     landed(halo_o[2:])
     imitated[...] = convolved(grid_o, taps, rows, depth, False).astype(BF16)
+    stores[0].start()
     finish(halo_o)
     for copy in pair[0]:
         copy.wait()
@@ -351,13 +374,20 @@
         total2 = total2 + far2[o].astype(F32)
     grad_one[...] = total1
     grad_two[...] = total2.T
+    stores[1].start()
+    stores[2].start()
 
     def got_back(i, carry):
         homeward(out_b, in_b, b_send, b_recv, i).wait_recv()
         return carry
 
-    lax.fori_loop(0, own, got_back, 0)
-    feat_grad[...] = dot(back, in_b[...].reshape(slots, width)).astype(BF16)
+    lax.fori_loop(0, pairs, got_back, 0)
+    middle = pairs * cap
+    early = dot(back[:, :middle], in_b[:pairs].reshape(middle, width))
+    lax.fori_loop(pairs, own, got_back, 0)
+    late = dot(back[:, middle:], in_b[pairs:].reshape(middle, width))
+    feat_grad[...] = (early + late).astype(BF16)
+    stores[3].start()
 
     def drained(i, carry):
         outward(out_f, in_f, f_send, f_recv, i).wait_send()
@@ -367,17 +397,22 @@
         return carry
 
     lax.fori_loop(0, own, drained, 0)
+    for copy in stores:
+        copy.wait()
 
 
 def handed_on(*refs):
-    count = len(refs) // 2
-    sems = refs[-1]
-    copies = [
-        pltpu.make_async_copy(refs[i], refs[count + i], sems.at[i]) for i in range(count)
-    ]
-    for copy in copies:
+    count = (len(refs) - 2) // 3
+    news, olds, held = refs[count : 2 * count], refs[:count], refs[2 * count : 3 * count]
+    in_sem, out_sem = refs[-2:]
+    reads = [pltpu.make_async_copy(olds[i], held[i], in_sem.at[i]) for i in range(count)]
+    writes = [pltpu.make_async_copy(held[i], news[i], out_sem.at[i]) for i in range(count)]
+    for copy in reads:
         copy.start()
-    for copy in copies:
+    for read, write in zip(reads, writes):
+        read.wait()
+        write.start()
+    for copy in writes:
         copy.wait()
 
 
@@ -391,7 +426,6 @@
     cap = 2 * tokens // n_ex
     block = hidden // n_dp
     half = n_dp // 2
-    vmem = pl.BlockSpec(memory_space=pltpu.VMEM)
     hbm = pl.BlockSpec(memory_space=pltpu.HBM)
     wide = pltpu.VMEM((n_ex, cap, width), BF16)
     thin = pltpu.VMEM((n_ex, cap, channels), BF16)
@@ -405,9 +439,15 @@
             jax.ShapeDtypeStruct((width, block), F32),
             jax.ShapeDtypeStruct((block, channels), F32),
         ),
-        in_specs=[vmem, vmem, vmem, hbm, hbm, hbm],
-        out_specs=(vmem,) * 4,
+        in_specs=[hbm] * 6,
+        out_specs=(hbm,) * 4,
         scratch_shapes=[
+            pltpu.VMEM((tokens, channels), BF16),
+            pltpu.VMEM((tokens, width), BF16),
+            pltpu.VMEM((width, block), F32),
+            pltpu.VMEM((block, channels), F32),
+            pltpu.VMEM((1, tokens), jnp.int32),
+            pltpu.VMEM((tokens, width), BF16),
             pltpu.VMEM((width, hidden), BF16),
             pltpu.VMEM((hidden, channels), BF16),
             pltpu.VMEM(taps.shape, BF16),
@@ -425,13 +465,13 @@
             pltpu.VMEM((half, channels, block), BF16),
             pltpu.VMEM((half, width, block), BF16),
             pltpu.VMEM((half, channels, block), BF16),
-            dma((3,)), dma((8,)), dma((8,)),
+            dma((6,)), dma((4,)), dma((8,)), dma((8,)),
             dma((n_ex,)), dma((n_ex,)), dma((n_ex,)), dma((n_ex,)),
             dma((n_ex,)), dma((n_ex,)), dma((n_ex,)), dma((n_ex,)),
             dma((2, half)), dma((2, half)), dma((2, half)), dma((2, half)),
         ],
         compiler_params=pltpu.CompilerParams(
-            collective_id=0, has_side_effects=True, vmem_limit_bytes=50 * 2**20
+            collective_id=0, has_side_effects=True, vmem_limit_bytes=60 * 2**20
         ),
         name="routed_experts",
     )(
@@ -445,10 +485,10 @@
     imitated, feat_grad, grad_one, grad_two = pl.pallas_call(
         handed_on,
         out_shape=tuple(jax.ShapeDtypeStruct(x.shape, x.dtype) for x in outs),
-        in_specs=[vmem] * 4,
+        in_specs=[hbm] * 4,
         out_specs=(hbm,) * 4,
-        scratch_shapes=[dma((4,))],
-        compiler_params=pltpu.CompilerParams(vmem_limit_bytes=8 * 2**20),
+        scratch_shapes=[pltpu.VMEM(x.shape, x.dtype) for x in outs] + [dma((4,)), dma((4,))],
+        compiler_params=pltpu.CompilerParams(vmem_limit_bytes=60 * 2**20),
         name="handed_on",
     )(*outs)
     return (

time: 92.3 us -> 102 us (1.11)
  the two profiles are of different devices: /device:TPU:17 before, /device:TPU:10 now
where the time goes in v2:
time: 102 us
  Pallas kernels  101 us (99%)
    pallas_call x1, Pallas kernels, per_device(): pl.pallas_call(functools.partial(kernel, n_dp, n_ex), out_shape=(jax.Shap...  98.5 us
    pallas_call x1, Pallas kernels, per_device(): pl.pallas_call(handed_on, out_shape=tuple((jax.ShapeDtypeStruct(x.shape,...  2.68 us

profile of v2, /device:TPU:10, one launch (start us, length us, event | category | flops | bytes accessed | tf_op | source)
XLA Modules:
  0.0 102.0 jit_solution(2173755814389130528)
XLA Ops:
  0.6 98.5 %routed_experts.1 = (bf16[512,256]{1,0:T(8,128)(2,1)}, bf16[512,512]{1,0:T(8,128)(2,1)}, f32[512,512]{1,0:T(8,128)}, f32[512,256]{1,0:T(8,128)}) custom-call(s32[1,512]{1,0:T(1,128)} %bitcast.13, bf16[512,512]{1,0:T(8,128)(2,1)} %bitcast.11, bf16[4,128,256]{2,1,0:T(8,128)(2,1)} %bitcast.12, bf16[512,2048]{1,0:T(8,128)(2,1)} %bitcast.9, ...), custom_call_target="tpu_custom_call" | custom-call | tf_op jit(solution)/shard_map/routed_experts/pallas_call | solution.py:434
  99.2 2.7 %handed_on.1 = (bf16[512,256]{1,0:T(8,128)(2,1)}, bf16[512,512]{1,0:T(8,128)(2,1)}, f32[512,512]{1,0:T(8,128)}, f32[512,256]{1,0:T(8,128)}) custom-call(bf16[512,256]{1,0:T(8,128)(2,1)} %get-tuple-element.12.refs_0_, bf16[512,512]{1,0:T(8,128)(2,1)} %get-tuple-element.13.refs_1_, f32[512,512]{1,0:T(8,128)} %get-tuple-element.14.refs_2_, ...), custom_call_target="tpu_custom_call" | custom-call | tf_op jit(solution)/shard_map/handed_on/pallas_call | solution.py:485

commit v3 on v2

--- a/solution.py
+++ b/solution.py
@@ -120,6 +120,13 @@
         )
         return carry
 
+    for x in (1, n_dp - 1):
+        for y in (1, n_ex - 1):
+            pl.semaphore_signal(
+                barrier, inc=1,
+                device_id={"dp": (dp + x) % n_dp, "expert": (me + y) % n_ex},
+                device_id_type=pl.DeviceIdType.MESH,
+            )
     lax.fori_loop(1, n_ex, greet_expert, 0)
     lax.fori_loop(1, n_dp, greet_dp, 0)
     loads[3].wait()
@@ -187,9 +194,35 @@
         def _():
             grid[rows + 1, 1] = strip
 
-    halo_g, halo_o = halo(grid_g, 0), halo(grid_o, 4)
+    def halo_at_once(grid, at):
+        inner = pl.ds(1, rows)
+        steps = []
+        for x in (-1, 0, 1):
+            for y in (-1, 0, 1):
+                if x == 0 and y == 0:
+                    continue
+                mine = {-1: 1, 0: inner, 1: rows}[y]
+                theirs = {-1: rows + 1, 0: inner, 1: 0}[y]
+                near = True
+                come = True
+                if x != 0:
+                    near = dp < n_dp - 1 if x > 0 else dp > 0
+                    come = dp > 0 if x > 0 else dp < n_dp - 1
+                if y != 0:
+                    goes = me < n_ex - 1 if y > 0 else me > 0
+                    gets = me > 0 if y > 0 else me < n_ex - 1
+                    near = goes if x == 0 else jnp.logical_and(near, goes)
+                    come = gets if x == 0 else jnp.logical_and(come, gets)
+                spot = at + len(steps)
+                steps.append((near, come, remote(
+                    grid.at[mine, 1], grid.at[theirs, 1 - x],
+                    halo_send.at[spot], halo_recv.at[spot],
+                    dp=(dp + x + n_dp) % n_dp, expert=(me + y + n_ex) % n_ex)))
+        return steps
+
+    halo_g, halo_o = halo(grid_g, 0), halo_at_once(grid_o, 4)
     loads[4].wait()
-    pl.semaphore_wait(barrier, n_ex + n_dp - 2)
+    pl.semaphore_wait(barrier, n_ex + n_dp + 2)
     begin(halo_g[:2])
     loads[5].wait()
 
@@ -219,6 +252,17 @@
     own = n_ex - 1
     lax.fori_loop(0, 2, send_feats, 0)
     edges(grid_g)
+    edges(grid_o)
+    strips = jnp.zeros((3, depth, channels), BF16)
+
+    @pl.when(me == 0)
+    def _():
+        grid_o[0] = strips
+
+    @pl.when(me == n_ex - 1)
+    def _():
+        grid_o[rows + 1] = strips
+
     landed(halo_g[:2])
     begin(halo_g[2:])
     lax.fori_loop(2, own, send_feats, 0)
@@ -261,12 +305,15 @@
         for i in (2 * k, 2 * k + 1):
             outward(out_f, in_f, f_send, f_recv, i).wait_recv()
         forward(k)
+        for i in (2 * k, 2 * k + 1):
+            homeward(out_o, in_o, o_send, o_recv, i).start()
         return carry
 
     pairs = n_ex // 2
     lax.fori_loop(0, pairs - 1, go_forward, 0)
     outward(out_f, in_f, f_send, f_recv, own - 1).wait_recv()
     forward(pairs - 1)
+    homeward(out_o, in_o, o_send, o_recv, own - 1).start()
     in_o[own] = out_o[own]
 
     def backward(k):
@@ -292,18 +339,9 @@
         backward(k)
         return carry
 
-    def send_outs(i, carry):
-        homeward(out_o, in_o, o_send, o_recv, i).start()
-        return carry
-
-    got_grads(0)
-    got_grads(1)
-    lax.fori_loop(0, own, send_outs, 0)
-    backward(0)
+    go_backward(0, 0)
     lax.fori_loop(0, 2, send_back, 0)
-    lax.fori_loop(1, pairs // 2, go_backward, 0)
-    lax.fori_loop(2, pairs, send_back, 0)
-    lax.fori_loop(pairs // 2, pairs - 1, go_backward, 0)
+    lax.fori_loop(1, pairs - 1, go_backward, 0)
     got_grads(own - 1)
     backward(pairs - 1)
     in_b[own] = out_b[own]
@@ -333,18 +371,14 @@
         homeward(out_o, in_o, o_send, o_recv, i).wait_recv()
         return carry
 
-    for o in range(1, half):
+    for o in list(range(1, half)) + [0]:
         weight_blocks(o)
     lax.fori_loop(0, own, got_outs, 0)
     back = spread[...].reshape(slots, tokens).T
     mixed = dot(back, in_o[...].reshape(slots, channels)).astype(BF16)
     grid_o[1 : rows + 1, 1] = mixed.reshape(rows, depth, channels)
-    begin(halo_o[:2])
-    lax.fori_loop(pairs, own, send_back, 0)
-    edges(grid_o)
-    weight_blocks(0)
-    landed(halo_o[:2])
-    begin(halo_o[2:])
+    begin(halo_o)
+    lax.fori_loop(2, own, send_back, 0)
     far = []
     for o in range(1, half):
         other = (level + o) % half
@@ -359,7 +393,7 @@
             sum2.at[o], far2.at[o], far_send.at[1, o], far_recv.at[1, o], dp=to))
         far[-2].start()
         far[-1].start()
-    landed(halo_o[2:])
+    landed(halo_o)
     imitated[...] = convolved(grid_o, taps, rows, depth, False).astype(BF16)
     stores[0].start()
     finish(halo_o)
@@ -465,7 +499,7 @@
             pltpu.VMEM((half, channels, block), BF16),
             pltpu.VMEM((half, width, block), BF16),
             pltpu.VMEM((half, channels, block), BF16),
-            dma((6,)), dma((4,)), dma((8,)), dma((8,)),
+            dma((6,)), dma((4,)), dma((12,)), dma((12,)),
             dma((n_ex,)), dma((n_ex,)), dma((n_ex,)), dma((n_ex,)),
             dma((n_ex,)), dma((n_ex,)), dma((n_ex,)), dma((n_ex,)),
             dma((2, half)), dma((2, half)), dma((2, half)), dma((2, half)),

time: 102 us -> 89.1 us (0.87); the launches traced: 102 us -> 88.1 us
  Pallas kernels: 101 us -> 87.3 us
    pallas_call x1, Pallas kernels: 98.5 us -> 84.6 us  [per_device(): pl.pallas_call(functools.partial(kernel, n_dp, n_ex), out_shape=(jax.Shap...]
where the time goes in v3:
time: 89.1 us; the launch traced here: 88.1 us
  Pallas kernels  87.3 us (98%)
    pallas_call x1, Pallas kernels, per_device(): pl.pallas_call(functools.partial(kernel, n_dp, n_ex), out_shape=(jax.Shap...  84.6 us
    pallas_call x1, Pallas kernels, per_device(): pl.pallas_call(handed_on, out_shape=tuple((jax.ShapeDtypeStruct(x.shape,...  2.68 us

profile of v3, /device:TPU:10, one launch (start us, length us, event | category | flops | bytes accessed | tf_op | source)
XLA Modules:
  0.0 88.1 jit_solution(924797639835393752)
XLA Ops:
  0.6 84.6 %routed_experts.1 = (bf16[512,256]{1,0:T(8,128)(2,1)}, bf16[512,512]{1,0:T(8,128)(2,1)}, f32[512,512]{1,0:T(8,128)}, f32[512,256]{1,0:T(8,128)}) custom-call(s32[1,512]{1,0:T(1,128)} %bitcast.13, bf16[512,512]{1,0:T(8,128)(2,1)} %bitcast.11, bf16[4,128,256]{2,1,0:T(8,128)(2,1)} %bitcast.12, bf16[512,2048]{1,0:T(8,128)(2,1)} %bitcast.9, ...), custom_call_target="tpu_custom_call" | custom-call | tf_op jit(solution)/shard_map/routed_experts/pallas_call | solution.py:468
  85.2 2.7 %handed_on.1 = (bf16[512,256]{1,0:T(8,128)(2,1)}, bf16[512,512]{1,0:T(8,128)(2,1)}, f32[512,512]{1,0:T(8,128)}, f32[512,256]{1,0:T(8,128)}) custom-call(bf16[512,256]{1,0:T(8,128)(2,1)} %get-tuple-element.12.refs_0_, bf16[512,512]{1,0:T(8,128)(2,1)} %get-tuple-element.13.refs_1_, f32[512,512]{1,0:T(8,128)} %get-tuple-element.14.refs_2_, ...), custom_call_target="tpu_custom_call" | custom-call | tf_op jit(solution)/shard_map/handed_on/pallas_call | solution.py:519

commit v4 on v3

--- a/solution.py
+++ b/solution.py
@@ -371,7 +371,7 @@
         homeward(out_o, in_o, o_send, o_recv, i).wait_recv()
         return carry
 
-    for o in list(range(1, half)) + [0]:
+    for o in range(1, half):
         weight_blocks(o)
     lax.fori_loop(0, own, got_outs, 0)
     back = spread[...].reshape(slots, tokens).T
@@ -393,6 +393,7 @@
             sum2.at[o], far2.at[o], far_send.at[1, o], far_recv.at[1, o], dp=to))
         far[-2].start()
         far[-1].start()
+    weight_blocks(0)
     landed(halo_o)
     imitated[...] = convolved(grid_o, taps, rows, depth, False).astype(BF16)
     stores[0].start()

time: 89.1 us -> 89.1 us (level)
  no operation moved by 1% of the time
where the time goes in v4:
time: 89.1 us; the launch traced here: 88.1 us
  Pallas kernels  87.3 us (98%)
    pallas_call x1, Pallas kernels, per_device(): pl.pallas_call(functools.partial(kernel, n_dp, n_ex), out_shape=(jax.Shap...  84.7 us
    pallas_call x1, Pallas kernels, per_device(): pl.pallas_call(handed_on, out_shape=tuple((jax.ShapeDtypeStruct(x.shape,...  2.68 us

profile of v4, /device:TPU:10, one launch (start us, length us, event | category | flops | bytes accessed | tf_op | source)
XLA Modules:
  0.0 88.1 jit_solution(16252336821653109347)
XLA Ops:
  0.6 84.7 %routed_experts.1 = (bf16[512,256]{1,0:T(8,128)(2,1)}, bf16[512,512]{1,0:T(8,128)(2,1)}, f32[512,512]{1,0:T(8,128)}, f32[512,256]{1,0:T(8,128)}) custom-call(s32[1,512]{1,0:T(1,128)} %bitcast.13, bf16[512,512]{1,0:T(8,128)(2,1)} %bitcast.11, bf16[4,128,256]{2,1,0:T(8,128)(2,1)} %bitcast.12, bf16[512,2048]{1,0:T(8,128)(2,1)} %bitcast.9, ...), custom_call_target="tpu_custom_call" | custom-call | tf_op jit(solution)/shard_map/routed_experts/pallas_call | solution.py:469
  85.3 2.7 %handed_on.1 = (bf16[512,256]{1,0:T(8,128)(2,1)}, bf16[512,512]{1,0:T(8,128)(2,1)}, f32[512,512]{1,0:T(8,128)}, f32[512,256]{1,0:T(8,128)}) custom-call(bf16[512,256]{1,0:T(8,128)(2,1)} %get-tuple-element.12.refs_0_, bf16[512,512]{1,0:T(8,128)(2,1)} %get-tuple-element.13.refs_1_, f32[512,512]{1,0:T(8,128)} %get-tuple-element.14.refs_2_, ...), custom_call_target="tpu_custom_call" | custom-call | tf_op jit(solution)/shard_map/handed_on/pallas_call | solution.py:520
